TPU v7x, 32 devices: a whole 2x2x4 slice. The times are simulated.
32 devices in a mesh: dp: 8 (over z, x), ctx: 4 (over y, core).
Axes of the slice: x: 2, y: 2, z: 4, core: 2. Of those that a mesh axis runs over, the one named last changes fastest.
Arguments:
- inputs: bfloat16 [16, 1024, 768], P('dp', 'ctx'), may hold values from -6 to 6
- encoded: bfloat16 [16, 512, 768], P('dp', 'ctx'), may hold values from -6 to 6
- cotangent: bfloat16 [16, 1024, 768], P('dp', 'ctx'), may hold values from -6 to 6
- norm_gains: float32 [3, 768], replicated, may hold values from 0.5 to 1.5
- rel_table: float32 [32, 12], replicated, may hold values from -4 to 4
- self_q: bfloat16 [768, 768], P('dp', 'ctx'), may hold values from -0.0390625 to 0.0390625
- self_kv: bfloat16 [2, 768, 768], P(None, 'dp', 'ctx'), may hold values from -0.21875 to 0.21875
- self_o: bfloat16 [768, 768], P('dp', 'ctx'), may hold values from -0.875 to 0.875
- cross_q: bfloat16 [768, 768], P('dp', 'ctx'), may hold values from -0.0390625 to 0.0390625
- cross_kv: bfloat16 [2, 768, 768], P(None, 'dp', 'ctx'), may hold values from -0.21875 to 0.21875
- cross_o: bfloat16 [768, 768], P('dp', 'ctx'), may hold values from -0.875 to 0.875
- ffn_in: bfloat16 [2, 768, 2048], P(None, 'dp', 'ctx'), may hold values from -0.21875 to 0.21875
- ffn_out: bfloat16 [2048, 768], P('dp', 'ctx'), may hold values from -0.125 to 0.125
- dec_segments: int32 [16, 1024], P('dp'), may hold values from 0 to 3, as said below
- enc_segments: int32 [16, 512], P('dp'), may hold values from 0 to 3, as said below
- rel_buckets: int32 [1024], replicated, may hold values from 0 to 31, as said below
Outputs:
- output: bfloat16 [16, 1024, 768], P('dp', 'ctx')
- d_inputs: bfloat16 [16, 1024, 768], P('dp', 'ctx')
- d_encoded: bfloat16 [16, 512, 768], P('dp', 'ctx')
- d_norm_gains: float32 [3, 768], replicated
- d_rel_table: float32 [32, 12], replicated
- d_self_q: float32 [768, 768], P('dp', 'ctx')
- d_self_kv: float32 [2, 768, 768], P(None, 'dp', 'ctx')
- d_self_o: float32 [768, 768], P('dp', 'ctx')
- d_cross_q: float32 [768, 768], P('dp', 'ctx')
- d_cross_kv: float32 [2, 768, 768], P(None, 'dp', 'ctx')
- d_cross_o: float32 [768, 768], P('dp', 'ctx')
- d_ffn_in: float32 [2, 768, 2048], P(None, 'dp', 'ctx')
- d_ffn_out: float32 [2048, 768], P('dp', 'ctx')
Inputs may be any that keep to these rules, and one draw needn't show every extreme that they name: `dec_segments`: along each sequence the numbers never fall, start at 0 and take every value up to that sequence's largest; a sequence's decoder and encoder tokens use the same set of numbers. In each aligned group of 2 sequences one sequence is a single document and another has four. `enc_segments`: along each sequence the numbers never fall, start at 0 and take every value up to that sequence's largest, the same set as the sequence's decoder tokens. `rel_buckets`: never falls with the distance; 0 at distance 0.
All inputs are finite; a program needn't handle non-finite values.
Results may differ from a plain program's by a relative error of at most 0.025.
The roundings to bfloat16 on the way count: a program that leaves them out, or rounds other values in their place, can miss the bound.
Values may be sent and summed in bfloat16 or wider, within the bound.
A program may use at most 320 MiB of HBM per device.

v0:
```python
import jax
import jax.numpy as jnp
from jax import lax
from jax.sharding import PartitionSpec as P

HEADS = 12


epsilon = 1e-06
masked_score = -1000000000.0
highest = lax.Precision.HIGHEST


def rms_norm(value, gain):
    return value * lax.rsqrt(jnp.mean(value * value, axis=-1, keepdims=True) + epsilon) * gain


def gated_unit(gate_value, up_value):
    return jax.nn.gelu(gate_value, approximate=True) * up_value


def split_heads(value):
    return value.reshape(value.shape[:-1] + (HEADS, value.shape[-1] // HEADS))


def merge_heads(value):
    return value.reshape(value.shape[:-2] + (value.shape[-2] * value.shape[-1],))


def gather_weights(shards):
    widened = (
        lax.all_gather(shards[0], "ctx", axis=1, tiled=True),
        lax.all_gather(shards[1], "ctx", axis=2, tiled=True),
        lax.all_gather(shards[2], "ctx", axis=1, tiled=True),
        lax.all_gather(shards[3], "ctx", axis=1, tiled=True),
        lax.all_gather(shards[4], "ctx", axis=2, tiled=True),
        lax.all_gather(shards[5], "ctx", axis=1, tiled=True),
        lax.all_gather(shards[6], "ctx", axis=2, tiled=True),
        lax.all_gather(shards[7], "ctx", axis=1, tiled=True),
    )
    return (
        lax.all_gather(widened[0], "dp", axis=0, tiled=True),
        lax.all_gather(widened[1], "dp", axis=1, tiled=True),
        lax.all_gather(widened[2], "dp", axis=0, tiled=True),
        lax.all_gather(widened[3], "dp", axis=0, tiled=True),
        lax.all_gather(widened[4], "dp", axis=1, tiled=True),
        lax.all_gather(widened[5], "dp", axis=0, tiled=True),
        lax.all_gather(widened[6], "dp", axis=1, tiled=True),
        lax.all_gather(widened[7], "dp", axis=0, tiled=True),
    )


def reduce_grads(whole):
    narrowed = (
        lax.psum_scatter(
            whole[0].astype(jnp.bfloat16), "dp", scatter_dimension=0, tiled=True
        ).astype(jnp.float32),
        lax.psum_scatter(
            whole[1].astype(jnp.bfloat16), "dp", scatter_dimension=1, tiled=True
        ).astype(jnp.float32),
        lax.psum_scatter(
            whole[2].astype(jnp.bfloat16), "dp", scatter_dimension=0, tiled=True
        ).astype(jnp.float32),
        lax.psum_scatter(
            whole[3].astype(jnp.bfloat16), "dp", scatter_dimension=0, tiled=True
        ).astype(jnp.float32),
        lax.psum_scatter(
            whole[4].astype(jnp.bfloat16), "dp", scatter_dimension=1, tiled=True
        ).astype(jnp.float32),
        lax.psum_scatter(
            whole[5].astype(jnp.bfloat16), "dp", scatter_dimension=0, tiled=True
        ).astype(jnp.float32),
        lax.psum_scatter(
            whole[6].astype(jnp.bfloat16), "dp", scatter_dimension=1, tiled=True
        ).astype(jnp.float32),
        lax.psum_scatter(
            whole[7].astype(jnp.bfloat16), "dp", scatter_dimension=0, tiled=True
        ).astype(jnp.float32),
    )
    return (
        lax.psum_scatter(
            narrowed[0].astype(jnp.bfloat16), "ctx", scatter_dimension=1, tiled=True
        ).astype(jnp.float32),
        lax.psum_scatter(
            narrowed[1].astype(jnp.bfloat16), "ctx", scatter_dimension=2, tiled=True
        ).astype(jnp.float32),
        lax.psum_scatter(
            narrowed[2].astype(jnp.bfloat16), "ctx", scatter_dimension=1, tiled=True
        ).astype(jnp.float32),
        lax.psum_scatter(
            narrowed[3].astype(jnp.bfloat16), "ctx", scatter_dimension=1, tiled=True
        ).astype(jnp.float32),
        lax.psum_scatter(
            narrowed[4].astype(jnp.bfloat16), "ctx", scatter_dimension=2, tiled=True
        ).astype(jnp.float32),
        lax.psum_scatter(
            narrowed[5].astype(jnp.bfloat16), "ctx", scatter_dimension=1, tiled=True
        ).astype(jnp.float32),
        lax.psum_scatter(
            narrowed[6].astype(jnp.bfloat16), "ctx", scatter_dimension=2, tiled=True
        ).astype(jnp.float32),
        lax.psum_scatter(
            narrowed[7].astype(jnp.bfloat16), "ctx", scatter_dimension=1, tiled=True
        ).astype(jnp.float32),
    )


def add_tuples(first, second):
    if first is None:
        return tuple(second)
    return tuple((left_item + right_item for left_item, right_item in zip(first, second)))


def score_block(queries, key_rows, score_bias, visible):
    scores = jnp.einsum("sphd,slhd->shpl", queries, key_rows, preferred_element_type=jnp.float32)
    scores = scores + score_bias
    return jnp.where(visible[:, None], scores, masked_score)


def attend_forward(queries, key_rows, value_rows, score_bias, visible):
    scores = score_block(queries, key_rows, score_bias, visible)
    row_max = jnp.max(scores, axis=-1, keepdims=True)
    exponent = jnp.exp(scores - row_max)
    row_total = jnp.sum(exponent, axis=-1, keepdims=True)
    attn_probs = (exponent / row_total).astype(jnp.bfloat16)
    mixed = jnp.einsum(
        "shpl,slhd->sphd", attn_probs, value_rows, preferred_element_type=jnp.float32
    )
    return (merge_heads(mixed).astype(jnp.bfloat16), row_max + jnp.log(row_total))


def attend_backward(queries, key_rows, value_rows, score_bias, visible, log_total, d_mixed):
    scores = score_block(queries, key_rows, score_bias, visible)
    attn_probs = jnp.exp(scores - log_total)
    d_probs = jnp.einsum("sphd,slhd->shpl", d_mixed, value_rows, preferred_element_type=jnp.float32)
    row_delta = jnp.sum(attn_probs * d_probs, axis=-1, keepdims=True)
    d_scores = (attn_probs * (d_probs - row_delta)).astype(jnp.bfloat16)
    d_queries = jnp.einsum(
        "shpl,slhd->sphd", d_scores, key_rows, preferred_element_type=jnp.float32
    )
    d_values = jnp.einsum(
        "shpl,sphd->slhd",
        attn_probs.astype(jnp.bfloat16),
        d_mixed,
        preferred_element_type=jnp.float32,
    )
    d_keys = jnp.einsum("shpl,sphd->slhd", d_scores, queries, preferred_element_type=jnp.float32)
    return (merge_heads(d_queries), merge_heads(d_keys), merge_heads(d_values), d_scores, row_delta)


def on_device(
    inputs,
    encoded,
    cotangent,
    norm_gains,
    rel_table,
    self_q,
    self_kv,
    self_o,
    cross_q,
    cross_kv,
    cross_o,
    ffn_in,
    ffn_out,
    dec_segments,
    enc_segments,
    rel_buckets,
):
    ctx_size = lax.axis_size("ctx")
    seq_dev = inputs.shape[0]
    pos_dev = inputs.shape[1]
    seq_len = dec_segments.shape[1]
    bucket_count = rel_table.shape[0]
    micro_count = max(2, seq_dev * 2 // ctx_size)
    seq_micro = seq_dev // micro_count
    ctx_start = lax.axis_index("ctx") * pos_dev
    query_place = ctx_start + jnp.arange(pos_dev, dtype=jnp.int32)
    key_place = jnp.arange(seq_len, dtype=jnp.int32)
    distance = jnp.maximum(query_place[:, None] - key_place[None, :], 0)
    causal = key_place[None, :] <= query_place[:, None]
    bucket_ids = jnp.arange(bucket_count, dtype=jnp.int32)
    bucket_hot = (rel_buckets[:, None] == bucket_ids[None, :]).astype(jnp.float32)
    dist_bias = jnp.dot(bucket_hot, rel_table, precision=highest).T
    score_bias = jnp.take(dist_bias, distance, axis=1)
    pair_hot = (jnp.take(rel_buckets, distance)[None] == bucket_ids[:, None, None]).astype(
        jnp.float32
    )
    shards = (self_q, self_kv, self_o, cross_q, cross_kv, cross_o, ffn_in, ffn_out)
    gain_grads = jnp.zeros_like(norm_gains)
    table_grads = jnp.zeros_like(rel_table)
    owned = None
    whole = None
    output_parts = []
    d_input_parts = []
    d_encoded_parts = []
    for micro_index in range(micro_count):
        lower = micro_index * seq_micro
        upper = lower + seq_micro
        hidden_in = inputs[lower:upper]
        enc_rows = encoded[lower:upper]
        cot_rows = cotangent[lower:upper]
        seg_keys = dec_segments[lower:upper]
        seg_enc = enc_segments[lower:upper]
        seg_query = lax.dynamic_slice_in_dim(seg_keys, ctx_start, pos_dev, 1)
        self_mask = (seg_query[:, :, None] == seg_keys[:, None, :]) & causal[None]
        cross_mask = seg_query[:, :, None] == seg_enc[:, None, :]
        full_weights = gather_weights(shards)
        (
            query_self,
            keyval_self,
            output_self,
            query_cross,
            keyval_cross,
            output_cross,
            ffn_inner,
            ffn_outer,
        ) = full_weights
        resid_in = hidden_in.astype(jnp.float32)
        normed_one = rms_norm(resid_in, norm_gains[0]).astype(jnp.bfloat16)
        queries_one = jnp.dot(normed_one, query_self, preferred_element_type=jnp.float32).astype(
            jnp.bfloat16
        )
        keyval_one = jnp.einsum(
            "spd,kde->kspe", normed_one, keyval_self, preferred_element_type=jnp.float32
        ).astype(jnp.bfloat16)
        keyval_two = jnp.einsum(
            "sed,kdf->ksef", enc_rows, keyval_cross, preferred_element_type=jnp.float32
        ).astype(jnp.bfloat16)
        keyval_one_all, keyval_two_all = (
            lax.all_gather(keyval_one, "ctx", axis=2, tiled=True),
            lax.all_gather(keyval_two, "ctx", axis=2, tiled=True),
        )
        keys_one = split_heads(keyval_one_all[0])
        values_one = split_heads(keyval_one_all[1])
        keys_two = split_heads(keyval_two_all[0])
        values_two = split_heads(keyval_two_all[1])
        attn_one, log_one = attend_forward(
            split_heads(queries_one), keys_one, values_one, score_bias, self_mask
        )
        resid_one = resid_in + jnp.dot(attn_one, output_self, preferred_element_type=jnp.float32)
        normed_two = rms_norm(resid_one, norm_gains[1]).astype(jnp.bfloat16)
        queries_two = jnp.dot(normed_two, query_cross, preferred_element_type=jnp.float32).astype(
            jnp.bfloat16
        )
        attn_two, log_two = attend_forward(
            split_heads(queries_two), keys_two, values_two, 0.0, cross_mask
        )
        resid_two = resid_one + jnp.dot(attn_two, output_cross, preferred_element_type=jnp.float32)
        normed_three = rms_norm(resid_two, norm_gains[2]).astype(jnp.bfloat16)
        gate_up = jnp.einsum(
            "spd,kdf->kspf", normed_three, ffn_inner, preferred_element_type=jnp.float32
        )
        middle = gated_unit(gate_up[0], gate_up[1]).astype(jnp.bfloat16)
        result = resid_two + jnp.dot(middle, ffn_outer, preferred_element_type=jnp.float32)
        output_parts.append(result.astype(jnp.bfloat16))
        grad_out = cot_rows.astype(jnp.float32)
        g_ffn_outer = jnp.einsum(
            "spf,spd->fd", middle, cot_rows, preferred_element_type=jnp.float32
        )
        d_middle = jnp.einsum(
            "spd,fd->spf", cot_rows, ffn_outer, preferred_element_type=jnp.float32
        )
        unit_out, unit_pull = jax.vjp(gated_unit, gate_up[0], gate_up[1])
        d_gate, d_up = unit_pull(d_middle)
        d_gate_up = jnp.stack([d_gate, d_up]).astype(jnp.bfloat16)
        g_ffn_inner = jnp.einsum(
            "spd,kspf->kdf", normed_three, d_gate_up, preferred_element_type=jnp.float32
        )
        d_normed_three = jnp.einsum(
            "kspf,kdf->spd", d_gate_up, ffn_inner, preferred_element_type=jnp.float32
        )
        norm_out, norm_pull = jax.vjp(rms_norm, resid_two, norm_gains[2])
        d_resid, d_gain_three = norm_pull(d_normed_three)
        d_resid_two = grad_out + d_resid
        d_cross_out = d_resid_two.astype(jnp.bfloat16)
        g_output_cross = jnp.einsum(
            "spd,spe->de", attn_two, d_cross_out, preferred_element_type=jnp.float32
        )
        d_attn_two = jnp.einsum(
            "spe,de->spd", d_cross_out, output_cross, preferred_element_type=jnp.float32
        ).astype(jnp.bfloat16)
        d_queries_two, d_keys_two, d_values_two, unused_scores, delta_two = attend_backward(
            split_heads(queries_two),
            keys_two,
            values_two,
            0.0,
            cross_mask,
            log_two,
            split_heads(d_attn_two),
        )
        d_queries_two = d_queries_two.astype(jnp.bfloat16)
        g_query_cross = jnp.einsum(
            "spd,spe->de", normed_two, d_queries_two, preferred_element_type=jnp.float32
        )
        d_normed_two = jnp.einsum(
            "spe,de->spd", d_queries_two, query_cross, preferred_element_type=jnp.float32
        )
        norm_out, norm_pull = jax.vjp(rms_norm, resid_one, norm_gains[1])
        d_resid, d_gain_two = norm_pull(d_normed_two)
        d_resid_one = d_resid_two + d_resid
        d_self_out = d_resid_one.astype(jnp.bfloat16)
        g_output_self = jnp.einsum(
            "spd,spe->de", attn_one, d_self_out, preferred_element_type=jnp.float32
        )
        d_attn_one = jnp.einsum(
            "spe,de->spd", d_self_out, output_self, preferred_element_type=jnp.float32
        ).astype(jnp.bfloat16)
        d_queries_one, d_keys_one, d_values_one, d_scores_one, delta_one = attend_backward(
            split_heads(queries_one),
            keys_one,
            values_one,
            score_bias,
            self_mask,
            log_one,
            split_heads(d_attn_one),
        )
        d_queries_one = d_queries_one.astype(jnp.bfloat16)
        score_sums = jnp.sum(d_scores_one, axis=0, dtype=jnp.float32)
        table_grads = table_grads + jnp.einsum(
            "bpl,hpl->bh", pair_hot, score_sums, precision=highest
        )
        d_keyval_one, d_keyval_two = (
            lax.psum_scatter(
                jnp.stack([d_keys_one, d_values_one]).astype(jnp.bfloat16),
                "ctx",
                scatter_dimension=2,
                tiled=True,
            ).astype(jnp.float32),
            lax.psum_scatter(
                jnp.stack([d_keys_two, d_values_two]).astype(jnp.bfloat16),
                "ctx",
                scatter_dimension=2,
                tiled=True,
            ).astype(jnp.float32),
        )
        d_keyval_one = d_keyval_one.astype(jnp.bfloat16)
        d_keyval_two = d_keyval_two.astype(jnp.bfloat16)
        g_query_self = jnp.einsum(
            "spd,spe->de", normed_one, d_queries_one, preferred_element_type=jnp.float32
        )
        g_keyval_self = jnp.einsum(
            "spd,kspe->kde", normed_one, d_keyval_one, preferred_element_type=jnp.float32
        )
        d_normed_one = jnp.einsum(
            "spe,de->spd", d_queries_one, query_self, preferred_element_type=jnp.float32
        )
        d_normed_one = d_normed_one + jnp.einsum(
            "kspe,kde->spd", d_keyval_one, keyval_self, preferred_element_type=jnp.float32
        )
        norm_out, norm_pull = jax.vjp(rms_norm, resid_in, norm_gains[0])
        d_resid, d_gain_one = norm_pull(d_normed_one)
        d_input_parts.append((d_resid_one + d_resid).astype(jnp.bfloat16))
        g_keyval_cross = jnp.einsum(
            "sed,ksef->kdf", enc_rows, d_keyval_two, preferred_element_type=jnp.float32
        )
        d_encoded_rows = jnp.einsum(
            "ksef,kdf->sed", d_keyval_two, keyval_cross, preferred_element_type=jnp.float32
        )
        d_encoded_parts.append(d_encoded_rows.astype(jnp.bfloat16))
        gain_grads = gain_grads + jnp.stack([d_gain_one, d_gain_two, d_gain_three])
        micro_grads = (
            g_query_self,
            g_keyval_self,
            g_output_self,
            g_query_cross,
            g_keyval_cross,
            g_output_cross,
            g_ffn_inner,
            g_ffn_outer,
        )
        whole = add_tuples(whole, micro_grads)
    owned = tuple(reduce_grads(whole))
    gain_total, table_total = lax.psum((gain_grads, table_grads), ("dp", "ctx"))
    return (
        jnp.concatenate(output_parts, axis=0),
        jnp.concatenate(d_input_parts, axis=0),
        jnp.concatenate(d_encoded_parts, axis=0),
        gain_total,
        table_total,
    ) + tuple(owned)


def solution(mesh):
    placed = (
        P("dp", "ctx", None),
        P("dp", "ctx", None),
        P("dp", "ctx", None),
        P(),
        P(),
        P("dp", "ctx"),
        P(None, "dp", "ctx"),
        P("dp", "ctx"),
        P("dp", "ctx"),
        P(None, "dp", "ctx"),
        P("dp", "ctx"),
        P(None, "dp", "ctx"),
        P("dp", "ctx"),
        P("dp", None),
        P("dp", None),
        P(),
    )
    return jax.shard_map(
        on_device,
        mesh=mesh,
        in_specs=placed,
        out_specs=(
            P("dp", "ctx", None),
            P("dp", "ctx", None),
            P("dp", "ctx", None),
            P(),
            P(),
            P("dp", "ctx"),
            P(None, "dp", "ctx"),
            P("dp", "ctx"),
            P("dp", "ctx"),
            P(None, "dp", "ctx"),
            P("dp", "ctx"),
            P(None, "dp", "ctx"),
            P("dp", "ctx"),
        ),
        check_vma=False,
    )
```

profile of v0, /device:TPU:0, one launch (start us, length us, event | category | flops | bytes accessed | tf_op | source)
XLA Modules:
  0.0 3040.4 jit_solution(17786375421383103218)
XLA Ops:
  8.3 7.9 all_gather.83
  18.4 6.6 all_gather.76
  26.1 5.6 all_gather.79
  32.6 37.7 %all-gather.21.cloned.1.call-done = bf16[2,768,768]{2,1,0:T(8,128)(2,1)} async-done(((bf16[2,96,768]{2,1,0:T(8,128)(2,1)}), bf16[2,768,768]{2,1,0:T(8,128)(2,1)}) %all-gather.21.cloned.1.call-update) | async-done | bytes 2359312 | tf_op jit(solution)/shard_map/all_gather | solution.py:46
  77.2 46.4 %all-gather.13.cloned.1.call-done = bf16[2,768,768]{2,1,0:T(8,128)(2,1)} async-done(((bf16[2,96,768]{2,1,0:T(8,128)(2,1)}), bf16[2,768,768]{2,1,0:T(8,128)(2,1)}) %all-gather.13.cloned.1.call-update) | async-done | bytes 2359312 | tf_op jit(solution)/shard_map/all_gather | solution.py:43
  127.2 5.6 all_gather.81
  133.8 5.6 all_gather.86
  143.9 5.7 all_gather.88
  150.6 9.2 all_gather.90
  159.8 7.0 all_gather.92
  168.2 862.0 %gather_fusion = f32[262144,12]{1,0:T(8,128)} fusion(f32[12,1024]{0,1:T(8,128)S(1)} %copy.182, s32[262144]{0:T(1024)S(1)} %broadcast_clamp_fusion), kind=kCustom, calls=%fused_computation | custom fusion | bytes 26214400 | tf_op jit(solution)/shard_map/jit(_take)/gather | solution.py:184
  1030.2 76.0 %copy.237 = f32[256,1024,12]{1,0,2:T(8,128)} copy(f32[256,1024,12]{2,1,0:T(8,128)} %bitcast.11) | data formatting | bytes 25165824 | tf_op jit(solution)/shard_map/jit(_take)/gather | solution.py:184
  1124.3 7.1 fusion.275
  1151.3 7.1 fusion.276
  1189.1 7.1 fusion.251
  1200.1 5.7 fusion.130
  1220.5 8.5 multiply_reduce_fusion.2
  1233.0 5.9 multiply_convert_fusion.2
  1241.4 5.0 copy.240
  1249.3 5.6 multiply_reduce_fusion.3
  1277.5 11.2 multiply_reduce_fusion.1
  1288.7 6.3 multiply_convert_fusion.1
  1306.0 12.1 multiply_reduce_fusion
  1318.2 6.6 multiply_convert_fusion
  1333.1 4.9 convolution_convert_fusion.10
  1339.6 4.8 convolution_convert_fusion.6
  1371.9 16.4 copy.222
  1411.3 43.8 %reduce-scatter.42.cloned.1.call-done = bf16[96,768]{1,0:T(8,128)(2,1)} async-done(((bf16[768,768]{1,0:T(8,128)(2,1)}), bf16[96,768]{1,0:T(8,128)(2,1)}) %reduce-scatter.42.cloned.1.call-update) | async-done | bytes 147472 | tf_op jit(solution)/shard_map/reduce_scatter | solution.py:55
  1456.9 64.5 %reduce-scatter.44.cloned.1.call-done = bf16[96,768]{1,0:T(8,128)(2,1)} async-done(((bf16[768,768]{1,0:T(8,128)(2,1)}), bf16[96,768]{1,0:T(8,128)(2,1)}) %reduce-scatter.44.cloned.1.call-update) | async-done | bytes 147472 | tf_op jit(solution)/shard_map/reduce_scatter | solution.py:61
  1523.2 1041.2 %gather_fusion.1 = s32[262144]{0:T(1024)S(1)} fusion(s32[1024]{0:T(1024)S(1)} %copy-done.3, s32[262144]{0:T(1024)S(1)} %copy-done.54), kind=kCustom, calls=%fused_computation.1 | custom fusion | bytes 3145728 | tf_op jit(solution)/shard_map/jit(_take)/gather | solution.py:185
  2566.5 12.0 copy.216
  2580.4 7.4 fusion.110
  2587.7 12.0 copy.217
  2601.6 7.7 fusion.112
  2611.6 4.8 fusion.98
  2620.6 29.6 copy.244
  2650.3 29.1 reshape.1497
  2690.4 29.6 copy.250
  2720.0 29.2 reshape.1503
  2755.4 77.2 %copy.254 = bf16[2,96,2048]{0,1,2:T(8,128)(2,1)} copy(bf16[2,96,2048]{2,0,1:T(2,128)(2,1)S(1)} %constant_dynamic-slice_fusion) | data formatting | bytes 1572864
  2832.5 71.4 %reshape.1507 = bf16[2048,192]{1,0:T(8,128)(2,1)} reshape(bf16[2048,96,2]{2,1,0:T(8,128)(2,1)} %bitcast.635) | data formatting | bytes 1572864
  2909.7 40.9 %all-reduce.3 = (f32[3,768]{1,0:T(4,128)}, f32[32,12]{0,1:T(8,128)}) all-reduce(f32[3,768]{1,0:T(4,128)S(1)} %maximum_add_fusion, f32[32,12]{0,1:T(8,128)S(1)} %fusion.112), channel_id=1, replica_groups=mesh['dp'=8,'ctx'=4] {'dp','ctx'}, use_global_device_ids=true, to_apply=%region_34.35 | all-reduce | flops 2688 | bytes 21504 | tf_op jit(solution)/shard_map/psum | solution.py:373
  2955.0 11.6 reshape.1498
  2966.6 5.6 copy.245
  2972.9 11.6 reshape.1504
  2984.5 5.6 copy.251
  2990.9 28.5 reshape.1508
  3019.3 13.1 copy.255
  (638 shorter events, 255.9 us)
Async XLA Ops:
  7.2 159.7 %copy-start = (f32[32,12]{0,1:T(8,128)S(1)}, f32[32,12]{0,1:T(8,128)}, u32[]{:S(2)}) copy-start(f32[32,12]{0,1:T(8,128)} %param.20) | copy-start | bytes 4612
  7.2 63.1 %copy-start.100 = (bf16[2,128,768]{2,1,0:T(8,128)(2,1)S(1)}, bf16[2,128,768]{2,1,0:T(8,128)(2,1)}, u32[]{:S(2)}) copy-start(bf16[2,128,768]{2,1,0:T(8,128)(2,1)} %param.17) | copy-start | bytes 1179652
  7.2 63.1 %all-gather.21.cloned.1.call-start = ((), (), s32[]{:S(2)}) async-start(), calls=%async_computation.21 | async-start | bytes 2654208 | tf_op jit(solution)/shard_map/all_gather | solution.py:46
  17.3 106.3 %all-gather.13.cloned.1.call-start = ((), (), s32[]{:S(2)}) async-start(), calls=%async_computation.17 | async-start | bytes 2654208 | tf_op jit(solution)/shard_map/all_gather | solution.py:43
  26.0 1083.5 %all-gather.17.cloned.1.call-start = ((), (), s32[]{:S(2)}) async-start(), calls=%async_computation.19 | async-start | bytes 1327104 | tf_op jit(solution)/shard_map/all_gather | solution.py:42
  32.6 1079.8 %all-gather.35.cloned.1.call-start = ((), (), s32[]{:S(2)}) async-start(), calls=%async_computation.28 | async-start | bytes 1966080 | tf_op jit(solution)/shard_map/all_gather | solution.py:231
  73.7 1041.4 %all-gather.23.cloned.1.call-start = ((), (), s32[]{:S(2)}) async-start(), calls=%async_computation.22 | async-start | bytes 1966080 | tf_op jit(solution)/shard_map/all_gather | solution.py:231
  75.4 1042.3 %all-gather.33.cloned.1.call-start = ((), (), s32[]{:S(2)}) async-start(), calls=%async_computation.27 | async-start | bytes 3932160 | tf_op jit(solution)/shard_map/all_gather | solution.py:230
  76.9 1034.7 %copy-start.130 = (f32[768]{0:T(1024)}, f32[768]{0:T(1024)S(1)}, u32[]{:S(2)}) copy-start(f32[768]{0:T(1024)S(1)} %get-tuple-element.82) | copy-start | bytes 9220
  77.1 50.0 %copy-start.164 = (f32[256]{0:T(256)}, f32[256]{0:T(256)S(1)}, u32[]{:S(2)}) copy-start(f32[256]{0:T(256)S(1)} %get-tuple-element.80) | copy-start | bytes 3076
  77.1 63.1 %copy-start.162 = (f32[256]{0:T(256)}, f32[256]{0:T(256)S(1)}, u32[]{:S(2)}) copy-start(f32[256]{0:T(256)S(1)} %get-tuple-element.79) | copy-start | bytes 3076
  77.1 49.9 %copy-start.140 = (bf16[96,192]{1,0:T(8,128)(2,1)S(1)}, bf16[96,192]{1,0:T(8,128)(2,1)}, u32[]{:S(2)}) copy-start(bf16[96,192]{1,0:T(8,128)(2,1)} %param.23) | copy-start | bytes 110596
  77.2 1032.3 %copy-start.154 = (f32[256]{0:T(256)}, f32[256]{0:T(256)S(1)}, u32[]{:S(2)}) copy-start(f32[256]{0:T(256)S(1)} %fusion.223) | copy-start | bytes 3076
  127.0 1012.6 %all-gather.19.cloned.1.call-start = ((), (), s32[]{:S(2)}) async-start(), calls=%async_computation.20 | async-start | bytes 1327104 | tf_op jit(solution)/shard_map/all_gather | solution.py:44
  133.6 1008.0 %all-gather.25.cloned.1.call-start = ((), (), s32[]{:S(2)}) async-start(), calls=%async_computation.23 | async-start | bytes 1327104 | tf_op jit(solution)/shard_map/all_gather | solution.py:45
  140.2 1004.4 %all-gather.15.cloned.1.call-start = ((), (), s32[]{:S(2)}) async-start(), calls=%async_computation.18 | async-start | bytes 3932160 | tf_op jit(solution)/shard_map/all_gather | solution.py:230
  140.3 971.3 %copy-start.148 = (f32[256]{0:T(256)}, f32[256]{0:T(256)S(1)}, u32[]{:S(2)}) copy-start(f32[256]{0:T(256)S(1)} %fusion.220) | copy-start | bytes 3076
  143.8 1033.0 %all-gather.27.cloned.1.call-start = ((), (), s32[]{:S(2)}) async-start(), calls=%async_computation.24 | async-start | bytes 1327104 | tf_op jit(solution)/shard_map/all_gather | solution.py:47
  150.5 1038.6 %all-gather.29.cloned.1.call-start = ((), (), s32[]{:S(2)}) async-start(), calls=%async_computation.25 | async-start | bytes 7077888 | tf_op jit(solution)/shard_map/all_gather | solution.py:48
  159.8 1040.3 %all-gather.31.cloned.1.call-start = ((), (), s32[]{:S(2)}) async-start(), calls=%async_computation.26 | async-start | bytes 3538944 | tf_op jit(solution)/shard_map/all_gather | solution.py:49
  166.9 1221.5 %reduce-scatter.54.cloned.1.call-start = ((), (), s32[]{:S(2)}) async-start(), calls=%async_computation.37 | async-start | bytes 1966080
  167.6 940.2 %copy-start.158 = (s32[256]{0:T(256)}, s32[256]{0:T(256)S(1)}, u32[]{:S(2)}) copy-start(s32[256]{0:T(256)S(1)} %iota_add_fusion) | copy-start | bytes 3076
  168.2 862.0 %copy-start.53 = (s32[262144]{0:T(1024)}, s32[262144]{0:T(1024)S(1)}, u32[]{:S(2)}) copy-start(s32[262144]{0:T(1024)S(1)} %broadcast_clamp_fusion) | copy-start | bytes 3145732
  1030.2 76.0 %copy-start.166 = (s32[2,1024]{1,0:T(2,128)S(1)}, s32[2,1024]{1,0:T(2,128)}, u32[]{:S(2)}) copy-start(s32[2,1024]{1,0:T(2,128)} %param.29) | copy-start | bytes 24580
  1030.2 76.1 %copy-start.173 = (s32[2,512]{1,0:T(2,128)S(1)}, s32[2,512]{1,0:T(2,128)}, u32[]{:S(2)}) copy-start(s32[2,512]{1,0:T(2,128)} %param.30) | copy-start | bytes 12292
  1167.4 94.8 %copy-start.143 = (f32[256]{0:T(256)}, f32[256]{0:T(256)S(1)}, u32[]{:S(2)}) copy-start(f32[256]{0:T(256)S(1)} %fusion.221) | copy-start | bytes 3076
  1249.2 140.8 %reduce-scatter.52.cloned.1.call-start = ((), (), s32[]{:S(2)}) async-start(), calls=%async_computation.36 | async-start | bytes 1966080
  1276.9 122.1 %reduce-scatter.38.cloned.1.call-start = ((), (), s32[]{:S(2)}) async-start(), calls=%async_computation.29 | async-start | bytes 3932160 | tf_op jit(solution)/shard_map/reduce_scatter | solution.py:323
  1302.0 101.1 %reduce-scatter.40.cloned.1.call-start = ((), (), s32[]{:S(2)}) async-start(), calls=%async_computation.30 | async-start | bytes 3932160 | tf_op jit(solution)/shard_map/reduce_scatter | solution.py:323
  1331.7 123.4 %reduce-scatter.42.cloned.1.call-start = ((), (), s32[]{:S(2)}) async-start(), calls=%async_computation.31 | async-start | bytes 1327104 | tf_op jit(solution)/shard_map/reduce_scatter | solution.py:55
  1346.1 175.3 %reduce-scatter.44.cloned.1.call-start = ((), (), s32[]{:S(2)}) async-start(), calls=%async_computation.32 | async-start | bytes 1327104 | tf_op jit(solution)/shard_map/reduce_scatter | solution.py:61
  1348.7 1229.9 %reduce-scatter.46.cloned.1.call-start = ((), (), s32[]{:S(2)}) async-start(), calls=%async_computation.33 | async-start | bytes 1327104 | tf_op jit(solution)/shard_map/reduce_scatter | solution.py:64
  1352.1 1247.6 %reduce-scatter.48.cloned.1.call-start = ((), (), s32[]{:S(2)}) async-start(), calls=%async_computation.34 | async-start | bytes 1327104 | tf_op jit(solution)/shard_map/reduce_scatter | solution.py:70
  1355.4 1254.0 %reduce-scatter.50.cloned.1.call-start = ((), (), s32[]{:S(2)}) async-start(), calls=%async_computation.35 | async-start | bytes 3538944 | tf_op jit(solution)/shard_map/reduce_scatter | solution.py:76
  1363.1 1256.1 %all-reduce.7.cloned.1.call-start = ((), (), s32[]{:S(2)}) async-start(), calls=%async_computation.46 | async-start | bytes 22020096
  1411.2 112.0 %copy-start.54 = (s32[262144]{0:T(1024)S(1)}, s32[262144]{0:T(1024)}, u32[]{:S(2)}) copy-start(s32[262144]{0:T(1024)} %copy-done.53) | copy-start | bytes 3145732
  1411.2 112.0 %copy-start.3 = (s32[1024]{0:T(1024)S(1)}, s32[1024]{0:T(1024)}, u32[]{:S(2)}) copy-start(s32[1024]{0:T(1024)} %param.31) | copy-start | bytes 12292
  1411.3 1270.4 %reduce-scatter.56.cloned.1.call-start = ((), (), s32[]{:S(2)}) async-start(), calls=%async_computation.38 | async-start | bytes 245760
  1456.9 1226.3 %reduce-scatter.60.cloned.1.call-start = ((), (), s32[]{:S(2)}) async-start(), calls=%async_computation.40 | async-start | bytes 245760
  1523.1 1161.6 %reduce-scatter.62.cloned.1.call-start = ((), (), s32[]{:S(2)}) async-start(), calls=%async_computation.41 | async-start | bytes 245760
  1523.2 1041.4 %copy-start.159 = (s32[256]{0:T(256)S(1)}, s32[256]{0:T(256)}, u32[]{:S(2)}) copy-start(s32[256]{0:T(256)} %copy-done.158) | copy-start | bytes 3076
  2580.3 106.0 %reduce-scatter.66.cloned.1.call-start = ((), (), s32[]{:S(2)}) async-start(), calls=%async_computation.43 | async-start | bytes 245760
  2601.5 351.7 %reduce-scatter.70.cloned.1.call-start = ((), (), s32[]{:S(2)}) async-start(), calls=%async_computation.45 | async-start | bytes 491520
  2611.3 343.6 %reduce-scatter.58.cloned.1.call-start = ((), (), s32[]{:S(2)}) async-start(), calls=%async_computation.39 | async-start | bytes 491520
  2679.4 293.5 %reduce-scatter.64.cloned.1.call-start = ((), (), s32[]{:S(2)}) async-start(), calls=%async_computation.42 | async-start | bytes 491520
  2749.3 241.6 %reduce-scatter.68.cloned.1.call-start = ((), (), s32[]{:S(2)}) async-start(), calls=%async_computation.44 | async-start | bytes 1310720
  2832.5 71.4 %copy-start.90 = (bf16[2,1,256,768]{2,3,0,1:T(8,128)(2,1)S(1)}, bf16[2,1,256,768]{2,3,0,1:T(8,128)(2,1)}, u32[]{:S(2)}) copy-start(bf16[2,1,256,768]{2,3,0,1:T(8,128)(2,1)} %reduce-scatter.38.cloned.1.call-done) | copy-start | bytes 2359300
  2907.9 42.7 %copy-start.40 = (f32[1,256,768]{2,1,0:T(8,128)S(1)}, f32[1,256,768]{2,1,0:T(8,128)}, u32[]{:S(2)}) copy-start(f32[1,256,768]{2,1,0:T(8,128)} %copy-done.38) | copy-start | bytes 2359300
  (169 other events, 1055.7 us)
Sparse Core Ops, SparseCore 0:
  17.4 52.8 all-gather.20
  73.1 50.4 all-gather.12
  126.3 39.5 all-gather.16
  167.9 18.5 all-gather.34
  188.6 19.8 all-gather.22
  210.4 28.5 all-gather.32
  241.8 41.0 all-gather.18
  285.6 39.8 all-gather.24
  327.0 27.2 all-gather.14
  356.4 41.0 all-gather.26
  399.7 97.7 all-gather.28
  499.4 61.2 all-gather.30
  1249.4 26.7 reduce-scatter.53
  1278.7 28.1 reduce-scatter.51
  1309.3 37.9 reduce-scatter.37
  1349.8 37.9 reduce-scatter.39
  1391.0 64.0 reduce-scatter.41
  1458.4 62.9 reduce-scatter.43
  1524.8 63.0 reduce-scatter.45
  1591.1 63.0 reduce-scatter.47
  1657.8 73.1 reduce-scatter.49
  1735.5 341.5 all-reduce.6
  2080.2 18.6 reduce-scatter.55
  2101.7 19.7 reduce-scatter.59
  2580.4 18.6 reduce-scatter.61
  2601.6 19.5 reduce-scatter.65
  2623.6 20.7 reduce-scatter.69
  2679.6 19.8 reduce-scatter.57
  2749.4 19.8 reduce-scatter.63
  2904.1 24.0 reduce-scatter.67
where the time goes:
time: 3050 us; the launch traced here: 3040 us
  local copies, waits for them, and re-layouts  2460 us (81%)
  matrix products  215 us (7%)
  waiting for transfers between devices  193 us (6%)
  blocking collectives  94.2 us (3%)
  other arithmetic  53.6 us (2%)
    gather x2, local copies, waits for them, and re-layouts, on_device(): jnp.take(rel_buckets, distance)[None] == bucket_ids[:, None, None]  1040 us
    gather x2, local copies, waits for them, and re-layouts, on_device(): score_bias = jnp.take(dist_bias, distance, axis=1)  938 us
    unnamed x418, local copies, waits for them, and re-layouts  401 us
    reduce_scatter x1, waiting for transfers between devices, reduce_grads(): lax.psum_scatter(whole[2].astype(jnp.bfloat16), 'dp', scatter_dimension=0...  64.5 us
  transfers between devices with their start and end apart: 30, of which 4 were waited for; matrix products, arithmetic and copies ran while one was open for 86% of the time, Pallas kernels for 0%

commit v1 on v0

v1 whole, which is shorter than its diff:
```python
import jax
import jax.numpy as jnp
from jax import lax
from jax.experimental import pallas as pl
from jax.experimental.pallas import tpu as pltpu
from jax.sharding import PartitionSpec as P

HEADS = 12


epsilon = 1e-06
masked_score = -1000000000.0
highest = lax.Precision.HIGHEST


def rms_norm(value, gain):
    return value * lax.rsqrt(jnp.mean(value * value, axis=-1, keepdims=True) + epsilon) * gain


def gated_unit(gate_value, up_value):
    return jax.nn.gelu(gate_value, approximate=True) * up_value


def split_heads(value):
    return value.reshape(value.shape[:-1] + (HEADS, value.shape[-1] // HEADS))


def merge_heads(value):
    return value.reshape(value.shape[:-2] + (value.shape[-2] * value.shape[-1],))


def project(value, weight):
    return jnp.einsum("spd,ed->spe", value, weight, preferred_element_type=jnp.float32).astype(
        jnp.bfloat16
    )


def pull_back(grad, weight):
    return jnp.einsum("spe,ed->spd", grad, weight, preferred_element_type=jnp.float32)


def weight_grad(value, grad):
    return jnp.einsum("spd,spe->ed", value, grad, preferred_element_type=jnp.float32)


def skew_kernel(row_ref, plane_ref):
    rows, columns = plane_ref.shape[1:]
    spread = jnp.broadcast_to(row_ref[0], (rows, row_ref.shape[2]))
    plane_ref[0] = pltpu.roll(spread, 0, 1, stride=1, stride_axis=0)[:, :columns]


def skew_rows(table_rows, rows, columns):
    count, width = table_rows.shape
    return pl.pallas_call(
        skew_kernel,
        grid=(count,),
        in_specs=[pl.BlockSpec((1, 1, width), lambda n: (n, 0, 0))],
        out_specs=pl.BlockSpec((1, rows, columns), lambda n: (n, 0, 0)),
        out_shape=jax.ShapeDtypeStruct((count, rows, columns), jnp.float32),
        compiler_params=pltpu.CompilerParams(vmem_limit_bytes=32 * 1024 * 1024),
    )(table_rows[:, None, :])


def gather_group(shards):
    widths = [shard.shape[1] for shard in shards]
    tall = lax.all_gather(jnp.concatenate(shards, axis=1), "dp", axis=0, tiled=True)
    flat = tall.T
    wholes = []
    lower = 0
    for width in widths:
        wholes.append(lax.all_gather(flat[lower : lower + width], "ctx", axis=0, tiled=True))
        lower += width
    return wholes


def reduce_group(grads):
    pieces = [
        lax.psum_scatter(grad.astype(jnp.bfloat16), "ctx", scatter_dimension=0, tiled=True)
        for grad in grads
    ]
    widths = [piece.shape[0] for piece in pieces]
    joined = jnp.concatenate(pieces, axis=0) if len(pieces) > 1 else pieces[0]
    owned = lax.psum_scatter(joined.T, "dp", scatter_dimension=0, tiled=True).astype(jnp.float32)
    blocks = []
    lower = 0
    for width in widths:
        blocks.append(owned[:, lower : lower + width])
        lower += width
    return blocks


def add_tuples(first, second):
    if first is None:
        return tuple(second)
    return tuple((left_item + right_item for left_item, right_item in zip(first, second)))


def score_block(queries, key_rows, score_bias, visible):
    scores = jnp.einsum("sphd,slhd->shpl", queries, key_rows, preferred_element_type=jnp.float32)
    scores = scores + score_bias
    return jnp.where(visible[:, None], scores, masked_score)


def attend_forward(queries, key_rows, value_rows, score_bias, visible):
    scores = score_block(queries, key_rows, score_bias, visible)
    row_max = jnp.max(scores, axis=-1, keepdims=True)
    exponent = jnp.exp(scores - row_max)
    row_total = jnp.sum(exponent, axis=-1, keepdims=True)
    attn_probs = (exponent / row_total).astype(jnp.bfloat16)
    mixed = jnp.einsum(
        "shpl,slhd->sphd", attn_probs, value_rows, preferred_element_type=jnp.float32
    )
    return (merge_heads(mixed).astype(jnp.bfloat16), row_max + jnp.log(row_total))


def attend_backward(queries, key_rows, value_rows, score_bias, visible, log_total, d_mixed):
    scores = score_block(queries, key_rows, score_bias, visible)
    attn_probs = jnp.exp(scores - log_total)
    d_probs = jnp.einsum("sphd,slhd->shpl", d_mixed, value_rows, preferred_element_type=jnp.float32)
    row_delta = jnp.sum(attn_probs * d_probs, axis=-1, keepdims=True)
    d_scores = (attn_probs * (d_probs - row_delta)).astype(jnp.bfloat16)
    d_queries = jnp.einsum(
        "shpl,slhd->sphd", d_scores, key_rows, preferred_element_type=jnp.float32
    )
    d_values = jnp.einsum(
        "shpl,sphd->slhd",
        attn_probs.astype(jnp.bfloat16),
        d_mixed,
        preferred_element_type=jnp.float32,
    )
    d_keys = jnp.einsum("shpl,sphd->slhd", d_scores, queries, preferred_element_type=jnp.float32)
    return (merge_heads(d_queries), merge_heads(d_keys), merge_heads(d_values), d_scores, row_delta)


def on_device(
    inputs,
    encoded,
    cotangent,
    norm_gains,
    rel_table,
    self_q,
    self_kv,
    self_o,
    cross_q,
    cross_kv,
    cross_o,
    ffn_in,
    ffn_out,
    dec_segments,
    enc_segments,
    rel_buckets,
):
    seq_dev = inputs.shape[0]
    pos_dev = inputs.shape[1]
    seq_len = dec_segments.shape[1]
    bucket_count = rel_table.shape[0]
    micro_count = max(1, seq_dev // 4)
    seq_micro = seq_dev // micro_count
    ctx_start = lax.axis_index("ctx") * pos_dev
    query_place = ctx_start + jnp.arange(pos_dev, dtype=jnp.int32)
    key_place = jnp.arange(seq_len, dtype=jnp.int32)
    causal = key_place[None, :] <= query_place[:, None]
    bucket_ids = jnp.arange(bucket_count, dtype=jnp.int32)
    width = -(-(pos_dev + seq_len) // 128) * 128
    offset = jnp.arange(width, dtype=jnp.int32)
    back = jnp.maximum(
        ctx_start + jnp.where(offset < seq_len, -offset, width - offset), 0
    )
    first_place = jnp.sum(
        (rel_buckets[None, :] < bucket_ids[:, None]).astype(jnp.int32), axis=1
    )
    row_bucket = (
        jnp.sum((back[None, :] >= first_place[:, None]).astype(jnp.int32), axis=0) - 1
    )
    bucket_hot = (row_bucket[:, None] == bucket_ids[None, :]).astype(jnp.float32)
    bias_rows = jnp.dot(bucket_hot, rel_table, precision=highest).T
    planes = skew_rows(
        jnp.concatenate([bias_rows, row_bucket[None].astype(jnp.float32)], axis=0),
        pos_dev,
        seq_len,
    )
    score_bias = planes[:HEADS]
    pair_hot = (planes[HEADS][None] == bucket_ids.astype(jnp.float32)[:, None, None]).astype(
        jnp.float32
    )
    query_self, key_self, value_self = gather_group([self_q, self_kv[0], self_kv[1]])
    key_cross, value_cross, output_self, query_cross, output_cross = gather_group(
        [cross_kv[0], cross_kv[1], self_o, cross_q, cross_o]
    )
    gate_inner, up_inner = gather_group([ffn_in[0], ffn_in[1]])
    (ffn_outer,) = gather_group([ffn_out])
    gain_grads = jnp.zeros_like(norm_gains)
    table_grads = jnp.zeros_like(rel_table)
    whole = None
    output_parts = []
    d_input_parts = []
    d_encoded_parts = []
    for micro_index in range(micro_count):
        lower = micro_index * seq_micro
        upper = lower + seq_micro
        hidden_in = inputs[lower:upper]
        enc_rows = encoded[lower:upper]
        cot_rows = cotangent[lower:upper]
        seg_keys = dec_segments[lower:upper]
        seg_enc = enc_segments[lower:upper]
        seg_query = lax.dynamic_slice_in_dim(seg_keys, ctx_start, pos_dev, 1)
        self_mask = (seg_query[:, :, None] == seg_keys[:, None, :]) & causal[None]
        cross_mask = seg_query[:, :, None] == seg_enc[:, None, :]
        resid_in = hidden_in.astype(jnp.float32)
        normed_one = rms_norm(resid_in, norm_gains[0]).astype(jnp.bfloat16)
        queries_one = jnp.einsum("spd,ed->spe", normed_one, query_self, preferred_element_type=jnp.float32).astype(
            jnp.bfloat16
        )
        keyval_one = jnp.stack([project(normed_one, key_self), project(normed_one, value_self)])
        keyval_two = jnp.stack([project(enc_rows, key_cross), project(enc_rows, value_cross)])
        keyval_one_all, keyval_two_all = (
            lax.all_gather(keyval_one, "ctx", axis=2, tiled=True),
            lax.all_gather(keyval_two, "ctx", axis=2, tiled=True),
        )
        keys_one = split_heads(keyval_one_all[0])
        values_one = split_heads(keyval_one_all[1])
        keys_two = split_heads(keyval_two_all[0])
        values_two = split_heads(keyval_two_all[1])
        attn_one, log_one = attend_forward(
            split_heads(queries_one), keys_one, values_one, score_bias, self_mask
        )
        resid_one = resid_in + jnp.einsum("spd,ed->spe", attn_one, output_self, preferred_element_type=jnp.float32)
        normed_two = rms_norm(resid_one, norm_gains[1]).astype(jnp.bfloat16)
        queries_two = jnp.einsum("spd,ed->spe", normed_two, query_cross, preferred_element_type=jnp.float32).astype(
            jnp.bfloat16
        )
        attn_two, log_two = attend_forward(
            split_heads(queries_two), keys_two, values_two, 0.0, cross_mask
        )
        resid_two = resid_one + jnp.einsum("spd,ed->spe", attn_two, output_cross, preferred_element_type=jnp.float32)
        normed_three = rms_norm(resid_two, norm_gains[2]).astype(jnp.bfloat16)
        gate_up = [
            jnp.einsum("spd,fd->spf", normed_three, inner, preferred_element_type=jnp.float32)
            for inner in (gate_inner, up_inner)
        ]
        middle = gated_unit(gate_up[0], gate_up[1]).astype(jnp.bfloat16)
        result = resid_two + jnp.einsum("spf,df->spd", middle, ffn_outer, preferred_element_type=jnp.float32)
        output_parts.append(result.astype(jnp.bfloat16))
        grad_out = cot_rows.astype(jnp.float32)
        g_ffn_outer = jnp.einsum(
            "spf,spd->df", middle, cot_rows, preferred_element_type=jnp.float32
        )
        d_middle = jnp.einsum(
            "spd,df->spf", cot_rows, ffn_outer, preferred_element_type=jnp.float32
        )
        unit_out, unit_pull = jax.vjp(gated_unit, gate_up[0], gate_up[1])
        d_gate, d_up = unit_pull(d_middle)
        d_gate = d_gate.astype(jnp.bfloat16)
        d_up = d_up.astype(jnp.bfloat16)
        g_gate_inner = weight_grad(normed_three, d_gate)
        g_up_inner = weight_grad(normed_three, d_up)
        d_normed_three = pull_back(d_gate, gate_inner) + pull_back(d_up, up_inner)
        norm_out, norm_pull = jax.vjp(rms_norm, resid_two, norm_gains[2])
        d_resid, d_gain_three = norm_pull(d_normed_three)
        d_resid_two = grad_out + d_resid
        d_cross_out = d_resid_two.astype(jnp.bfloat16)
        g_output_cross = weight_grad(attn_two, d_cross_out)
        d_attn_two = pull_back(d_cross_out, output_cross).astype(jnp.bfloat16)
        d_queries_two, d_keys_two, d_values_two, unused_scores, delta_two = attend_backward(
            split_heads(queries_two),
            keys_two,
            values_two,
            0.0,
            cross_mask,
            log_two,
            split_heads(d_attn_two),
        )
        d_queries_two = d_queries_two.astype(jnp.bfloat16)
        g_query_cross = weight_grad(normed_two, d_queries_two)
        d_normed_two = pull_back(d_queries_two, query_cross)
        norm_out, norm_pull = jax.vjp(rms_norm, resid_one, norm_gains[1])
        d_resid, d_gain_two = norm_pull(d_normed_two)
        d_resid_one = d_resid_two + d_resid
        d_self_out = d_resid_one.astype(jnp.bfloat16)
        g_output_self = weight_grad(attn_one, d_self_out)
        d_attn_one = pull_back(d_self_out, output_self).astype(jnp.bfloat16)
        d_queries_one, d_keys_one, d_values_one, d_scores_one, delta_one = attend_backward(
            split_heads(queries_one),
            keys_one,
            values_one,
            score_bias,
            self_mask,
            log_one,
            split_heads(d_attn_one),
        )
        d_queries_one = d_queries_one.astype(jnp.bfloat16)
        score_sums = jnp.sum(d_scores_one, axis=0, dtype=jnp.float32)
        table_grads = table_grads + jnp.einsum(
            "bpl,hpl->bh", pair_hot, score_sums, precision=highest
        )
        d_keyval_one, d_keyval_two = (
            lax.psum_scatter(
                jnp.stack([d_keys_one, d_values_one]).astype(jnp.bfloat16),
                "ctx",
                scatter_dimension=2,
                tiled=True,
            ).astype(jnp.float32),
            lax.psum_scatter(
                jnp.stack([d_keys_two, d_values_two]).astype(jnp.bfloat16),
                "ctx",
                scatter_dimension=2,
                tiled=True,
            ).astype(jnp.float32),
        )
        d_keyval_one = d_keyval_one.astype(jnp.bfloat16)
        d_keyval_two = d_keyval_two.astype(jnp.bfloat16)
        g_query_self = weight_grad(normed_one, d_queries_one)
        g_key_self = weight_grad(normed_one, d_keyval_one[0])
        g_value_self = weight_grad(normed_one, d_keyval_one[1])
        d_normed_one = pull_back(d_queries_one, query_self)
        d_normed_one = (
            d_normed_one
            + pull_back(d_keyval_one[0], key_self)
            + pull_back(d_keyval_one[1], value_self)
        )
        norm_out, norm_pull = jax.vjp(rms_norm, resid_in, norm_gains[0])
        d_resid, d_gain_one = norm_pull(d_normed_one)
        d_input_parts.append((d_resid_one + d_resid).astype(jnp.bfloat16))
        g_key_cross = weight_grad(enc_rows, d_keyval_two[0])
        g_value_cross = weight_grad(enc_rows, d_keyval_two[1])
        d_encoded_rows = pull_back(d_keyval_two[0], key_cross) + pull_back(
            d_keyval_two[1], value_cross
        )
        d_encoded_parts.append(d_encoded_rows.astype(jnp.bfloat16))
        gain_grads = gain_grads + jnp.stack([d_gain_one, d_gain_two, d_gain_three])
        micro_grads = (
            g_ffn_outer,
            g_gate_inner,
            g_up_inner,
            g_output_cross,
            g_query_cross,
            g_output_self,
            g_key_cross,
            g_value_cross,
            g_query_self,
            g_key_self,
            g_value_self,
        )
        whole = add_tuples(whole, micro_grads)
    (o_ffn_outer,) = reduce_group(whole[:1])
    o_ffn_inner = jnp.stack(reduce_group(whole[1:3]))
    o_output_cross, o_query_cross, o_output_self = reduce_group(whole[3:6])
    o_key_cross, o_value_cross, o_query_self, o_key_self, o_value_self = reduce_group(whole[6:])
    owned = (
        o_query_self,
        jnp.stack([o_key_self, o_value_self]),
        o_output_self,
        o_query_cross,
        jnp.stack([o_key_cross, o_value_cross]),
        o_output_cross,
        o_ffn_inner,
        o_ffn_outer,
    )
    gain_total, table_total = lax.psum((gain_grads, table_grads), ("dp", "ctx"))
    return (
        jnp.concatenate(output_parts, axis=0),
        jnp.concatenate(d_input_parts, axis=0),
        jnp.concatenate(d_encoded_parts, axis=0),
        gain_total,
        table_total,
    ) + owned


def solution(mesh):
    placed = (
        P("dp", "ctx", None),
        P("dp", "ctx", None),
        P("dp", "ctx", None),
        P(),
        P(),
        P("dp", "ctx"),
        P(None, "dp", "ctx"),
        P("dp", "ctx"),
        P("dp", "ctx"),
        P(None, "dp", "ctx"),
        P("dp", "ctx"),
        P(None, "dp", "ctx"),
        P("dp", "ctx"),
        P("dp", None),
        P("dp", None),
        P(),
    )
    return jax.shard_map(
        on_device,
        mesh=mesh,
        in_specs=placed,
        out_specs=(
            P("dp", "ctx", None),
            P("dp", "ctx", None),
            P("dp", "ctx", None),
            P(),
            P(),
            P("dp", "ctx"),
            P(None, "dp", "ctx"),
            P("dp", "ctx"),
            P("dp", "ctx"),
            P(None, "dp", "ctx"),
            P("dp", "ctx"),
            P(None, "dp", "ctx"),
            P("dp", "ctx"),
        ),
        check_vma=False,
    )
```

time: 3050 us -> 1260 us (0.41)
  local copies, waits for them, and re-layouts: 2460 us -> 128 us
  waiting for transfers between devices: 193 us -> 709 us
    gather x4 -> x0, local copies, waits for them, and re-layouts: 1980 us -> none  [the longest x2 1040 us: on_device(): jnp.take(rel_buckets, distance)[None] == bucket_ids[:, None, None]]
    unnamed x418 -> x200, local copies, waits for them, and re-layouts: 401 us -> 45.4 us
    reduce_scatter x5 -> x12, waiting for transfers between devices: 108 us -> 312 us  [the longest x10 254 us: reduce_group(): lax.psum_scatter(grad.astype(jnp.bfloat16), 'ctx', scatter_dimension=0, t...]
    unnamed x41 -> x36, waiting for transfers between devices: 0.53 us -> 178 us
    convert_element_type x13 -> x5, local copies, waits for them, and re-layouts: 58.1 us -> 5.31 us  [the longest x1 2.43 us: on_device(): jnp.einsum('spd,ed->spe', normed_two, query_cross, preferred_element_type...]
    all_gather x8 -> x13, waiting for transfers between devices: 84.2 us -> 137 us  [the longest x2 85.4 us: gather_group(): lax.all_gather(jnp.concatenate(shards, axis=1), 'dp', axis=0, tiled=True)]
    all_gather x2 -> x1, waiting for transfers between devices: 0.01 us -> 44.1 us  [on_device(): lax.all_gather(keyval_one, 'ctx', axis=2, tiled=True)]
    all_gather x8 -> x2, blocking collectives: 53.3 us -> 66.4 us  [gather_group(): lax.all_gather(jnp.concatenate(shards, axis=1), 'dp', axis=0, tiled=True)]
  transfers between devices with their start and end apart: 30 -> 32, of which waited for: 4 -> 22; matrix products, arithmetic and copies ran while one was open for 86% -> 26% of each run, Pallas kernels for 0% -> 0%
where the time goes in v1:
time: 1260 us; the launch traced here: 1250 us
  waiting for transfers between devices  709 us (56%)
  matrix products  218 us (17%)
  local copies, waits for them, and re-layouts  128 us (10%)
  blocking collectives  107 us (8%)
  other arithmetic  67 us (5%)
  between operations  15.7 us (1%)
    reduce_scatter x10, waiting for transfers between devices, reduce_group(): lax.psum_scatter(grad.astype(jnp.bfloat16), 'ctx', scatter_dimension=0, t...  254 us
    unnamed x36, waiting for transfers between devices  178 us
    all_gather x2, waiting for transfers between devices, gather_group(): lax.all_gather(jnp.concatenate(shards, axis=1), 'dp', axis=0, tiled=True)  85.4 us
    all_gather x2, blocking collectives, gather_group(): lax.all_gather(jnp.concatenate(shards, axis=1), 'dp', axis=0, tiled=True)  66.4 us
    reduce_scatter x1, waiting for transfers between devices, reduce_group(): lax.psum_scatter(joined.T, 'dp', scatter_dimension=0, tiled=True)  58 us
    all_gather x11, waiting for transfers between devices, gather_group(): lax.all_gather(flat[lower:lower + width], 'ctx', axis=0, tiled=True)  51.4 us
    unnamed x200, local copies, waits for them, and re-layouts  45.4 us
    all_gather x1, waiting for transfers between devices, on_device(): lax.all_gather(keyval_one, 'ctx', axis=2, tiled=True)  44.1 us
  transfers between devices with their start and end apart: 32, of which 22 were waited for; matrix products, arithmetic and copies ran while one was open for 26% of the time, Pallas kernels for 0%

profile of v1, /device:TPU:0, one launch (start us, length us, event | category | flops | bytes accessed | tf_op | source)
XLA Modules:
  0.0 1250.2 jit_solution(13753438433143164619)
XLA Ops:
  9.8 47.9 %all-gather.24.cloned.1.call-done = bf16[768,960]{1,0:T(8,128)(2,1)} async-done(((bf16[96,960]{1,0:T(8,128)(2,1)}), bf16[768,960]{1,0:T(8,128)(2,1)}) %all-gather.24.cloned.1.call-update) | async-done | bytes 1474576 | tf_op jit(solution)/shard_map/all_gather | solution.py:66
  61.7 32.7 %all_gather.51 = bf16[768,576]{1,0:T(8,128)(2,1)S(1)} all-gather(bf16[96,576]{1,0:T(8,128)(2,1)S(1)} %pad_maximum_fusion.8), channel_id=1, replica_groups=mesh['dp'=8,'ctx'=4] {'dp'}, dimensions={0}, use_global_device_ids=true | all-gather | bytes 995328 | tf_op jit(solution)/shard_map/all_gather | solution.py:66
  98.2 33.7 %all_gather.66 = bf16[2048,192]{0,1:T(8,128)(2,1)} all-gather(bf16[256,192]{0,1:T(8,128)(2,1)S(1)} %copy-done.58), channel_id=1, replica_groups=mesh['dp'=8,'ctx'=4] {'dp'}, dimensions={0}, use_global_device_ids=true | all-gather | bytes 884736 | tf_op jit(solution)/shard_map/all_gather | solution.py:66
  145.1 37.6 %all-gather.38.cloned.1.call-done = bf16[768,1024]{1,0:T(8,128)(2,1)} async-done(((bf16[96,1024]{1,0:T(8,128)(2,1)}), bf16[768,1024]{1,0:T(8,128)(2,1)}) %all-gather.38.cloned.1.call-update) | async-done | bytes 1572880 | tf_op jit(solution)/shard_map/all_gather | solution.py:66
  189.8 4.8 copy-done.1
  194.6 12.0 slice.168
  212.5 18.7 %all-gather.44.cloned.1.call-done = bf16[768,2048]{1,0:T(8,128)(2,1)} async-done(((bf16[192,2048]{1,0:T(8,128)(2,1)}), bf16[768,2048]{1,0:T(8,128)(2,1)}) %all-gather.44.cloned.1.call-update) | async-done | bytes 3145744 | tf_op jit(solution)/shard_map/all_gather | solution.py:71
  231.2 5.7 fusion.25
  236.9 25.4 %all-gather.32.cloned.1.call-done = bf16[2,2,512,768]{2,3,1,0:T(8,128)(2,1)} async-done(((bf16[2,2,128,768]{2,3,1,0:T(8,128)(2,1)}), bf16[2,2,512,768]{2,3,1,0:T(8,128)(2,1)}) %all-gather.32.cloned.1.call-update) | async-done | bytes 3145744 | tf_op jit(solution)/shard_map/all_gather | solution.py:218
  266.1 44.1 %all-gather.20.cloned.1.call-done = bf16[2,2,1024,768]{3,2,1,0:T(8,128)(2,1)} async-done(((bf16[2,2,256,768]{3,2,1,0:T(8,128)(2,1)}), bf16[2,2,1024,768]{3,2,1,0:T(8,128)(2,1)}) %all-gather.20.cloned.1.call-update) | async-done | bytes 6291472 | tf_op jit(solution)/shard_map/all_gather | solution.py:217
  310.1 5.9 fusion.109
  319.4 5.5 copy.162
  324.9 15.0 %fusion.115 = (f32[2,12,256]{2,1,0:T(8,128)}, f32[2,12,256,1024]{3,2,1,0:T(8,128)}) fusion(f32[12,256,1024]{2,1,0:T(8,128)} %slice.168, bf16[2,256,12,64]{1,3,2,0:T(8,128)(2,1)} %bitcast.259, bf16[2,1024,12,64]{1,3,2,0:T(8,128)(2,1)S(1)} %bitcast.251, pred[2,256,1024]{2,1,0:T(8,128)(4,1)} %compare_and_fusion), kind=kOutput, calls=%fused_computation.219 | convolution fusion | flops 824174592 | bytes 42229760 | tf_op jit(solution)/shard_map/sphd,slhd->shpl/dot_general | solution.py:99
  339.8 11.3 fusion.2
  351.2 10.8 fusion.60
  379.3 5.4 fusion.59
  388.9 8.3 all-gather.42.cloned.1.call-done
  397.2 5.7 fusion.31
  402.9 24.3 %all-gather.40.cloned.1.call-done = bf16[2048,768]{1,0:T(8,128)(2,1)} async-done(((bf16[512,768]{1,0:T(8,128)(2,1)}), bf16[2048,768]{1,0:T(8,128)(2,1)}) %all-gather.40.cloned.1.call-update) | async-done | bytes 3145744 | tf_op jit(solution)/shard_map/all_gather | solution.py:71
  427.1 9.2 fusion.24
  446.9 7.8 fusion.43
  454.7 10.4 multiply_reduce_fusion.1
  465.1 6.8 multiply_convert_fusion.1
  492.9 12.7 %fusion.38 = bf16[2,12,64,1024]{3,2,1,0:T(8,128)(2,1)} fusion(bf16[2,256,12,64]{1,3,2,0:T(8,128)(2,1)S(1)} %bitcast.263, f32[2,12,256,1024]{3,2,1,0:T(8,128)} %get-tuple-element.113, f32[2,12,256]{2,1,0:T(8,128)S(1)} %copy-done.46), kind=kOutput, calls=%fused_computation.75 | convolution fusion | flops 819462144 | bytes 29122560 | tf_op jit(solution)/shard_map/shpl,sphd->slhd/dot_general | solution.py:125
  510.3 16.5 %multiply_reduce_fusion = (f32[2,12,256]{2,1,0:T(8,128)}, f32[2,12,256,1024]{3,2,1,0:T(8,128)}) fusion(f32[2,12,256,1024]{3,2,1,0:T(8,128)} %get-tuple-element.113, f32[2,12,256]{2,1,0:T(8,128)} %log_add_fusion, bf16[2,256,12,64]{1,3,2,0:T(8,128)(2,1)} %bitcast.264, bf16[2,1024,12,64]{1,3,2,0:T(8,128)(2,1)S(1)} %bitcast.257), kind=kOutput, calls=%fused_computation.4 | convolution fusion | flops 824174592 | bytes 54312960 | tf_op jit(solution)/shard_map/sphd,slhd->shpl/dot_general | solution.py:119
  526.8 22.2 %convert_reduce_fusion = (f32[12,256,1024]{2,1,0:T(8,128)}, bf16[2,12,256,1024]{3,2,1,0:T(8,128)(2,1)S(1)}) fusion(f32[2,12,256,1024]{3,2,1,0:T(8,128)} %get-tuple-element.125, f32[2,12,256]{2,1,0:T(8,128)} %get-tuple-element.124, f32[2,12,256,1024]{3,2,1,0:T(8,128)} %get-tuple-element.113, f32[2,12,256]{2,1,0:T(8,128)} %log_add_fusion), kind=kLoop, calls=%fused_computation.2 | loop fusion | flops 34603008 | bytes 75546624 | tf_op jit(solution)/shard_map/reduce_sum | solution.py:292
  549.1 5.6 convolution_convert_fusion
  559.5 5.1 pad_maximum_fusion
  598.8 8.6 convolution_convert_fusion.8
  610.3 13.2 %reduce-scatter.26.cloned.1.call-done = bf16[2,2,256,768]{3,2,1,0:T(8,128)(2,1)} async-done(((bf16[2,2,1024,768]{3,2,1,0:T(8,128)(2,1)}), bf16[2,2,256,768]{3,2,1,0:T(8,128)(2,1)}) %reduce-scatter.26.cloned.1.call-update) | async-done | bytes 1572880 | tf_op jit(solution)/shard_map/reduce_scatter | solution.py:297
  628.8 22.9 %reduce-scatter.40.cloned.1.call-done = bf16[192,768]{1,0:T(8,128)(2,1)} async-done(((bf16[768,768]{1,0:T(8,128)(2,1)}), bf16[192,768]{1,0:T(8,128)(2,1)}) %reduce-scatter.40.cloned.1.call-update) | async-done | bytes 294928 | tf_op jit(solution)/shard_map/reduce_scatter | solution.py:78
  651.7 28.5 %reduce-scatter.42.cloned.1.call-done = bf16[192,768]{1,0:T(8,128)(2,1)} async-done(((bf16[768,768]{1,0:T(8,128)(2,1)}), bf16[192,768]{1,0:T(8,128)(2,1)}) %reduce-scatter.42.cloned.1.call-update) | async-done | bytes 294928 | tf_op jit(solution)/shard_map/reduce_scatter | solution.py:78
  680.1 28.2 %reduce-scatter.44.cloned.1.call-done = bf16[192,768]{1,0:T(8,128)(2,1)} async-done(((bf16[768,768]{1,0:T(8,128)(2,1)}), bf16[192,768]{1,0:T(8,128)(2,1)}) %reduce-scatter.44.cloned.1.call-update) | async-done | bytes 294928 | tf_op jit(solution)/shard_map/reduce_scatter | solution.py:78
  710.9 38.1 %reduce-scatter.58.cloned.1.call-done = bf16[192,2048]{1,0:T(8,128)(2,1)} async-done(((bf16[768,2048]{1,0:T(8,128)(2,1)}), bf16[192,2048]{1,0:T(8,128)(2,1)}) %reduce-scatter.58.cloned.1.call-update) | async-done | bytes 786448
  751.3 38.2 %reduce-scatter.46.cloned.1.call-done = bf16[512,768]{1,0:T(8,128)(2,1)} async-done(((bf16[2048,768]{1,0:T(8,128)(2,1)}), bf16[512,768]{1,0:T(8,128)(2,1)}) %reduce-scatter.46.cloned.1.call-update) | async-done | bytes 786448 | tf_op jit(solution)/shard_map/reduce_scatter | solution.py:78
  789.5 40.7 %reduce-scatter.48.cloned.1.call-done = bf16[512,768]{1,0:T(8,128)(2,1)} async-done(((bf16[2048,768]{1,0:T(8,128)(2,1)}), bf16[512,768]{1,0:T(8,128)(2,1)}) %reduce-scatter.48.cloned.1.call-update) | async-done | bytes 786448 | tf_op jit(solution)/shard_map/reduce_scatter | solution.py:78
  837.5 15.9 %copy.179 = f32[12,256,1024]{1,0,2:T(8,128)} copy(f32[12,256,1024]{2,1,0:T(8,128)} %get-tuple-element.76) | data formatting | bytes 25165824 | tf_op jit(solution)/shard_map/reduce_sum | solution.py:292
  853.4 19.4 %fusion.86 = f32[32,12]{0,1:T(8,128)S(1)} fusion(f32[12,256,1024]{1,0,2:T(8,128)} %copy.179, f32[256,1024]{0,1:T(8,128)S(1)} %copy.178, f32[32]{0:T(128)S(1)} %iota_convert_fusion), kind=kOutput, calls=%fused_computation.143 | convolution fusion | flops 1216348160 | bytes 13633152 | tf_op jit(solution)/shard_map/bpl,hpl->bh/dot_general | solution.py:293
  873.8 13.3 %reduce-scatter.32.cloned.1.call-done = bf16[192,768]{1,0:T(8,128)(2,1)} async-done(((bf16[768,768]{1,0:T(8,128)(2,1)}), bf16[192,768]{1,0:T(8,128)(2,1)}) %reduce-scatter.32.cloned.1.call-update) | async-done | bytes 294928 | tf_op jit(solution)/shard_map/reduce_scatter | solution.py:78
  888.0 27.2 %reduce-scatter.34.cloned.1.call-done = bf16[192,768]{1,0:T(8,128)(2,1)} async-done(((bf16[768,768]{1,0:T(8,128)(2,1)}), bf16[192,768]{1,0:T(8,128)(2,1)}) %reduce-scatter.34.cloned.1.call-update) | async-done | bytes 294928 | tf_op jit(solution)/shard_map/reduce_scatter | solution.py:78
  916.2 27.4 %reduce-scatter.36.cloned.1.call-done = bf16[192,768]{1,0:T(8,128)(2,1)} async-done(((bf16[768,768]{1,0:T(8,128)(2,1)}), bf16[192,768]{1,0:T(8,128)(2,1)}) %reduce-scatter.36.cloned.1.call-update) | async-done | bytes 294928 | tf_op jit(solution)/shard_map/reduce_scatter | solution.py:78
  944.5 27.3 %reduce-scatter.38.cloned.1.call-done = bf16[192,768]{1,0:T(8,128)(2,1)} async-done(((bf16[768,768]{1,0:T(8,128)(2,1)}), bf16[192,768]{1,0:T(8,128)(2,1)}) %reduce-scatter.38.cloned.1.call-update) | async-done | bytes 294928 | tf_op jit(solution)/shard_map/reduce_scatter | solution.py:78
  976.7 5.4 add_convert_fusion
  985.2 53.8 %reduce-scatter.54.cloned.1.call-done = bf16[96,576]{1,0:T(8,128)(2,1)} async-done(((bf16[768,576]{1,0:T(8,128)(2,1)}), bf16[96,576]{1,0:T(8,128)(2,1)}) %reduce-scatter.54.cloned.1.call-update) | async-done | bytes 110608
  1046.8 58.0 %reduce-scatter.50.cloned.1.call-done = bf16[256,192]{1,0:T(8,128)(2,1)} async-done(((bf16[2048,192]{1,0:T(8,128)(2,1)}), bf16[256,192]{1,0:T(8,128)(2,1)}) %reduce-scatter.50.cloned.1.call-update) | async-done | bytes 98320 | tf_op jit(solution)/shard_map/reduce_scatter | solution.py:83
  1106.5 66.0 %reduce-scatter.56.cloned.1.call-done = bf16[96,1024]{1,0:T(8,128)(2,1)} async-done(((bf16[768,1024]{1,0:T(8,128)(2,1)}), bf16[96,1024]{1,0:T(8,128)(2,1)}) %reduce-scatter.56.cloned.1.call-update) | async-done | bytes 196624
  1180.7 40.7 %all-reduce = (f32[3,768]{1,0:T(4,128)}, f32[32,12]{0,1:T(8,128)}) all-reduce(f32[3,768]{1,0:T(4,128)S(1)} %pad_maximum_fusion.10, f32[32,12]{0,1:T(8,128)S(1)} %fusion.86), channel_id=1, replica_groups=mesh['dp'=8,'ctx'=4] {'dp','ctx'}, use_global_device_ids=true, to_apply=%region_19.20 | all-reduce | flops 2688 | bytes 21504 | tf_op jit(solution)/shard_map/psum | solution.py:359
  1224.1 15.8 %reduce-scatter.52.cloned.1.call-done = bf16[96,960]{1,0:T(8,128)(2,1)} async-done(((bf16[768,960]{1,0:T(8,128)(2,1)}), bf16[96,960]{1,0:T(8,128)(2,1)}) %reduce-scatter.52.cloned.1.call-update) | async-done | bytes 184336
  (378 shorter events, 195.3 us)
Async XLA Ops:
  7.2 124.8 %copy-start = (bf16[2,128,768]{2,1,0:T(8,128)(2,1)S(1)}, bf16[2,128,768]{2,1,0:T(8,128)(2,1)}, u32[]{:S(2)}) copy-start(bf16[2,128,768]{2,1,0:T(8,128)(2,1)} %param.17) | copy-start | bytes 1179652
  7.2 50.5 %all-gather.24.cloned.1.call-start = ((), (), s32[]{:S(2)}) async-start(), calls=%async_computation.21 | async-start | bytes 1769472 | tf_op jit(solution)/shard_map/all_gather | solution.py:66
  9.8 122.2 %all-gather.28.cloned.1.call-start = ((), (), s32[]{:S(2)}) async-start(), calls=%async_computation.23 | async-start | bytes 1474560 | tf_op jit(solution)/shard_map/all_gather | solution.py:71
  60.8 73.0 %all-gather.30.cloned.1.call-start = ((), (), s32[]{:S(2)}) async-start(), calls=%async_computation.24 | async-start | bytes 1474560 | tf_op jit(solution)/shard_map/all_gather | solution.py:71
  61.5 75.8 %all-gather.16.cloned.1.call-start = ((), (), s32[]{:S(2)}) async-start(), calls=%async_computation.17 | async-start | bytes 1474560 | tf_op jit(solution)/shard_map/all_gather | solution.py:71
  96.0 43.5 %all-gather.18.cloned.1.call-start = ((), (), s32[]{:S(2)}) async-start(), calls=%async_computation.18 | async-start | bytes 1474560 | tf_op jit(solution)/shard_map/all_gather | solution.py:71
  96.6 86.1 %all-gather.38.cloned.1.call-start = ((), (), s32[]{:S(2)}) async-start(), calls=%async_computation.28 | async-start | bytes 1769472 | tf_op jit(solution)/shard_map/all_gather | solution.py:66
  97.4 111.7 %all-gather.22.cloned.1.call-start = ((), (), s32[]{:S(2)}) async-start(), calls=%async_computation.20 | async-start | bytes 1474560 | tf_op jit(solution)/shard_map/all_gather | solution.py:71
  98.1 133.1 %all-gather.44.cloned.1.call-start = ((), (), s32[]{:S(2)}) async-start(), calls=%async_computation.31 | async-start | bytes 3932160 | tf_op jit(solution)/shard_map/all_gather | solution.py:71
  131.9 130.4 %all-gather.32.cloned.1.call-start = ((), (), s32[]{:S(2)}) async-start(), calls=%async_computation.25 | async-start | bytes 3932160 | tf_op jit(solution)/shard_map/all_gather | solution.py:218
  136.6 173.6 %all-gather.20.cloned.1.call-start = ((), (), s32[]{:S(2)}) async-start(), calls=%async_computation.19 | async-start | bytes 7864320 | tf_op jit(solution)/shard_map/all_gather | solution.py:217
  137.0 72.1 %copy-start.60 = (f32[768]{0:T(1024)}, f32[768]{0:T(1024)S(1)}, u32[]{:S(2)}) copy-start(f32[768]{0:T(1024)S(1)} %get-tuple-element.72) | copy-start | bytes 9220
  137.3 71.8 %copy-start.63 = (f32[2,256]{1,0:T(2,128)}, f32[2,256]{1,0:T(2,128)S(1)}, u32[]{:S(2)}) copy-start(f32[2,256]{1,0:T(2,128)S(1)} %fusion.97) | copy-start | bytes 6148
  143.0 219.0 %all-gather.26.cloned.1.call-start = ((), (), s32[]{:S(2)}) async-start(), calls=%async_computation.22 | async-start | bytes 1474560 | tf_op jit(solution)/shard_map/all_gather | solution.py:71
  143.7 221.4 %all-gather.34.cloned.1.call-start = ((), (), s32[]{:S(2)}) async-start(), calls=%async_computation.26 | async-start | bytes 1474560 | tf_op jit(solution)/shard_map/all_gather | solution.py:71
  144.3 240.5 %all-gather.36.cloned.1.call-start = ((), (), s32[]{:S(2)}) async-start(), calls=%async_computation.27 | async-start | bytes 1474560 | tf_op jit(solution)/shard_map/all_gather | solution.py:71
  145.0 252.1 %all-gather.42.cloned.1.call-start = ((), (), s32[]{:S(2)}) async-start(), calls=%async_computation.30 | async-start | bytes 3932160 | tf_op jit(solution)/shard_map/all_gather | solution.py:71
  185.7 241.5 %all-gather.40.cloned.1.call-start = ((), (), s32[]{:S(2)}) async-start(), calls=%async_computation.29 | async-start | bytes 3932160 | tf_op jit(solution)/shard_map/all_gather | solution.py:71
  211.3 19.9 %copy-start.44 = (bf16[2,256,768]{2,1,0:T(8,128)(2,1)S(1)}, bf16[2,256,768]{2,1,0:T(8,128)(2,1)}, u32[]{:S(2)}) copy-start(bf16[2,256,768]{2,1,0:T(8,128)(2,1)} %param.18) | copy-start | bytes 2359300
  212.5 380.9 %reduce-scatter.28.cloned.1.call-start = ((), (), s32[]{:S(2)}) async-start(), calls=%async_computation.33 | async-start | bytes 3932160 | tf_op jit(solution)/shard_map/reduce_scatter | solution.py:303
  364.5 20.3 %copy-start.13 = (f32[2,256,768]{2,1,0:T(8,128)}, f32[2,256,768]{2,1,0:T(8,128)S(1)}, u32[]{:S(2)}) copy-start(f32[2,256,768]{2,1,0:T(8,128)S(1)} %get-tuple-element.115) | copy-start | bytes 4718596
  387.2 55.1 %copy-start.11 = (f32[2,256,768]{2,1,0:T(8,128)}, f32[2,256,768]{2,1,0:T(8,128)S(1)}, u32[]{:S(2)}) copy-start(f32[2,256,768]{2,1,0:T(8,128)S(1)} %get-tuple-element.119) | copy-start | bytes 4718596
  387.3 50.9 %copy-start.67 = (f32[2,256]{1,0:T(2,128)}, f32[2,256]{1,0:T(2,128)S(1)}, u32[]{:S(2)}) copy-start(f32[2,256]{1,0:T(2,128)S(1)} %fusion.99) | copy-start | bytes 6148
  388.9 38.3 %copy-start.42 = (bf16[2,256,768]{2,1,0:T(8,128)(2,1)}, bf16[2,256,768]{2,1,0:T(8,128)(2,1)S(1)}, u32[]{:S(2)}) copy-start(bf16[2,256,768]{2,1,0:T(8,128)(2,1)S(1)} %multiply_convert_fusion.4) | copy-start | bytes 2359300
  443.7 45.8 %copy-start.9 = (f32[2,256,768]{2,1,0:T(8,128)}, f32[2,256,768]{2,1,0:T(8,128)S(1)}, u32[]{:S(2)}) copy-start(f32[2,256,768]{2,1,0:T(8,128)S(1)} %fusion.48) | copy-start | bytes 4718596
  446.9 18.2 %slice-start = ((s8[12582912]{0:T(1024)(128)(4,1)}), s8[4194304]{0:T(1024)(128)(4,1)S(1)}, s32[]{:S(2)}) async-start(s8[12582912]{0:T(1024)(128)(4,1)} %bitcast.249), calls=%async_computation.49 | async-start | bytes 8388608
  446.9 18.2 %slice-start.1 = ((s8[12582912]{0:T(1024)(128)(4,1)}), s8[4194304]{0:T(1024)(128)(4,1)S(1)}, s32[]{:S(2)}) async-start(s8[12582912]{0:T(1024)(128)(4,1)} %bitcast.249), calls=%async_computation.50 | async-start | bytes 8388608
  485.0 138.5 %reduce-scatter.26.cloned.1.call-start = ((), (), s32[]{:S(2)}) async-start(), calls=%async_computation.32 | async-start | bytes 7864320 | tf_op jit(solution)/shard_map/reduce_scatter | solution.py:297
  564.7 87.0 %reduce-scatter.40.cloned.1.call-start = ((), (), s32[]{:S(2)}) async-start(), calls=%async_computation.39 | async-start | bytes 1474560 | tf_op jit(solution)/shard_map/reduce_scatter | solution.py:78
  569.1 111.1 %reduce-scatter.42.cloned.1.call-start = ((), (), s32[]{:S(2)}) async-start(), calls=%async_computation.40 | async-start | bytes 1474560 | tf_op jit(solution)/shard_map/reduce_scatter | solution.py:78
  572.3 136.0 %reduce-scatter.44.cloned.1.call-start = ((), (), s32[]{:S(2)}) async-start(), calls=%async_computation.41 | async-start | bytes 1474560 | tf_op jit(solution)/shard_map/reduce_scatter | solution.py:78
  576.0 173.0 %reduce-scatter.58.cloned.1.call-start = ((), (), s32[]{:S(2)}) async-start(), calls=%async_computation.48 | async-start | bytes 3932160
  582.8 206.7 %reduce-scatter.46.cloned.1.call-start = ((), (), s32[]{:S(2)}) async-start(), calls=%async_computation.42 | async-start | bytes 3932160 | tf_op jit(solution)/shard_map/reduce_scatter | solution.py:78
  588.2 242.0 %reduce-scatter.48.cloned.1.call-start = ((), (), s32[]{:S(2)}) async-start(), calls=%async_computation.43 | async-start | bytes 3932160 | tf_op jit(solution)/shard_map/reduce_scatter | solution.py:78
  593.3 279.5 %reduce-scatter.30.cloned.1.call-start = ((), (), s32[]{:S(2)}) async-start(), calls=%async_computation.34 | async-start | bytes 1474560 | tf_op jit(solution)/shard_map/reduce_scatter | solution.py:78
  595.9 291.1 %reduce-scatter.32.cloned.1.call-start = ((), (), s32[]{:S(2)}) async-start(), calls=%async_computation.35 | async-start | bytes 1474560 | tf_op jit(solution)/shard_map/reduce_scatter | solution.py:78
  598.7 316.4 %reduce-scatter.34.cloned.1.call-start = ((), (), s32[]{:S(2)}) async-start(), calls=%async_computation.36 | async-start | bytes 1474560 | tf_op jit(solution)/shard_map/reduce_scatter | solution.py:78
  608.3 15.2 %copy-start.26 = (bf16[2,256,768]{2,1,0:T(8,128)(2,1)S(1)}, bf16[2,256,768]{2,1,0:T(8,128)(2,1)}, u32[]{:S(2)}) copy-start(bf16[2,256,768]{2,1,0:T(8,128)(2,1)} %param.16) | copy-start | bytes 2359300
  610.3 333.3 %reduce-scatter.36.cloned.1.call-start = ((), (), s32[]{:S(2)}) async-start(), calls=%async_computation.37 | async-start | bytes 1474560 | tf_op jit(solution)/shard_map/reduce_scatter | solution.py:78
  626.8 345.1 %reduce-scatter.38.cloned.1.call-start = ((), (), s32[]{:S(2)}) async-start(), calls=%async_computation.38 | async-start | bytes 1474560 | tf_op jit(solution)/shard_map/reduce_scatter | solution.py:78
  628.8 410.2 %reduce-scatter.54.cloned.1.call-start = ((), (), s32[]{:S(2)}) async-start(), calls=%async_computation.46 | async-start | bytes 1105920
  710.9 393.9 %reduce-scatter.50.cloned.1.call-start = ((), (), s32[]{:S(2)}) async-start(), calls=%async_computation.44 | async-start | bytes 1179648 | tf_op jit(solution)/shard_map/reduce_scatter | solution.py:83
  751.3 421.2 %reduce-scatter.56.cloned.1.call-start = ((), (), s32[]{:S(2)}) async-start(), calls=%async_computation.47 | async-start | bytes 1769472
  833.4 406.5 %reduce-scatter.52.cloned.1.call-start = ((), (), s32[]{:S(2)}) async-start(), calls=%async_computation.45 | async-start | bytes 1769472
  983.2 60.5 %copy-start.34 = (bf16[2,2,128,768]{3,2,1,0:T(8,128)(2,1)S(1)}, bf16[2,2,128,768]{3,2,1,0:T(8,128)(2,1)}, u32[]{:S(2)}) copy-start(bf16[2,2,128,768]{3,2,1,0:T(8,128)(2,1)} %reduce-scatter.28.cloned.1.call-done) | copy-start | bytes 2359300
  985.2 58.6 %copy-start.33 = (bf16[768,768]{1,0:T(8,128)(2,1)S(1)}, bf16[768,768]{1,0:T(8,128)(2,1)}, u32[]{:S(2)}) copy-start(bf16[768,768]{1,0:T(8,128)(2,1)} %all-gather.28.cloned.1.call-done) | copy-start | bytes 3538948
  1177.1 44.3 %copy-start.66 = (f32[2,256]{1,0:T(2,128)S(1)}, f32[2,256]{1,0:T(2,128)}, u32[]{:S(2)}) copy-start(f32[2,256]{1,0:T(2,128)} %copy-done.65) | copy-start | bytes 6148
  1177.1 44.3 %copy-start.8 = (f32[2,256,768]{2,1,0:T(8,128)S(1)}, f32[2,256,768]{2,1,0:T(8,128)}, u32[]{:S(2)}) copy-start(f32[2,256,768]{2,1,0:T(8,128)} %copy-done.6) | copy-start | bytes 4718596
  (74 other events, 317.1 us)
Sparse Core Ops, SparseCore 0:
  10.8 46.8 all-gather.23
  60.9 16.2 all-gather.27
  79.4 17.4 all-gather.29
  98.9 17.4 all-gather.15
  118.3 17.4 all-gather.17
  138.4 44.1 all-gather.37
  184.8 16.2 all-gather.21
  202.7 28.5 all-gather.43
  233.4 28.9 all-gather.31
  263.7 46.3 all-gather.19
  311.7 17.4 all-gather.25
  330.6 17.4 all-gather.33
  349.7 17.4 all-gather.35
  368.6 28.5 all-gather.41
  398.6 28.5 all-gather.39
  485.1 37.9 reduce-scatter.27
  564.8 58.6 reduce-scatter.25
  625.9 25.6 reduce-scatter.39
  654.4 25.7 reduce-scatter.41
  682.6 25.7 reduce-scatter.43
  711.0 37.9 reduce-scatter.57
  751.6 37.9 reduce-scatter.45
  792.3 37.9 reduce-scatter.47
  832.7 25.7 reduce-scatter.29
  861.1 25.8 reduce-scatter.31
  889.4 25.6 reduce-scatter.33
  917.8 25.7 reduce-scatter.35
  946.1 25.6 reduce-scatter.37
  975.5 63.4 reduce-scatter.53
  1042.2 62.5 reduce-scatter.49
  1108.6 63.7 reduce-scatter.55
  1175.9 63.9 reduce-scatter.51
